TPU v7x, 32 devices: a whole 2x2x4 slice. The times are simulated.
32 devices in a mesh: row: 4 (over y, x), col: 4 (over z), depth: 2 (over core).
Axes of the slice: x: 2, y: 2, z: 4, core: 2. Of those that a mesh axis runs over, the one named last changes fastest.
Arguments:
- x_blocks: float32 [48, 16, 128, 128], P(('row', 'depth'), 'col'), may hold values from -1.2 to 1.2
- x_cols: int32 [48, 16], P(('row', 'depth'), 'col'), may hold values from 0 to 11, as said below
- c_cols: int32 [48, 16], P(('row', 'depth'), 'col'), may hold values from 0 to 11, as said below
Outputs:
- c_blocks: float32 [48, 16, 128, 128], P(('row', 'depth'), 'col')
Inputs may be any that keep to these rules, and one draw needn't show every extreme that they name: `x_cols`: within one block row and column tile the 4 entries are distinct. `c_cols`: within one block row and column tile the 4 entries are distinct.
All inputs are finite; a program needn't handle non-finite values.
Results may differ from a plain program's by a relative error of at most 0.0003.
Values sent between devices are 32-bit elements; how exact they have to be, the bound alone decides.
A program may use at most 128 MiB of HBM per device.

v0:
```python
import jax
import jax.numpy as jnp
from jax import lax
from jax.sharding import PartitionSpec as P


def from_behind(value, axis, steps):
    count = lax.axis_size(axis)
    pairs = [(source, (source + steps) % count) for source in range(count)]
    return lax.ppermute(value, axis, pairs)


def block_product(left_blocks, left_cols, right_blocks, right_cols, out_cols):
    picked = jnp.take(right_blocks, left_cols, axis=0)
    picked_cols = jnp.take(right_cols, left_cols, axis=0)
    partial_prod = jnp.einsum(
        "isab,istbc->istac", left_blocks, picked, precision=lax.Precision.HIGHEST
    )
    matches = (picked_cols[:, :, :, None] == out_cols[:, None, None, :]).astype(jnp.float32)
    return jnp.einsum("istu,istac->iuac", matches, partial_prod, precision=lax.Precision.HIGHEST)


def align_left(operand, distance, loop_size):
    for bit_index in range(loop_size.bit_length() - 1):
        arrived = from_behind((operand[0], operand[1]), "col", 1 << bit_index)
        chosen = distance >> bit_index & 1 == 1
        operand = (
            jnp.where(chosen, arrived[0], operand[0]),
            jnp.where(chosen, arrived[1], operand[1]),
        )
    return operand


def align_right(operand, distance, loop_size):
    for bit_index in range(loop_size.bit_length() - 1):
        arrived = from_behind((operand[0], operand[1]), "row", 1 << bit_index)
        chosen = distance >> bit_index & 1 == 1
        operand = (
            jnp.where(chosen, arrived[0], operand[0]),
            jnp.where(chosen, arrived[1], operand[1]),
        )
    return operand


def per_device(x_blocks, x_cols, c_cols):
    loop_size = lax.axis_size("col")
    layer_count = lax.axis_size("depth")
    row_index = lax.axis_index("row")
    col_index = lax.axis_index("col")
    layer_index = lax.axis_index("depth")
    full_blocks, full_cols, full_kept = (
        lax.all_gather(x_blocks, "depth", axis=0, tiled=True),
        lax.all_gather(x_cols, "depth", axis=0, tiled=True),
        lax.all_gather(c_cols, "depth", axis=0, tiled=True),
    )
    turn_count = loop_size // layer_count
    offset = layer_index * turn_count
    left_pair = (full_blocks, full_cols)
    right_pair = (full_blocks, full_cols)
    left_pair = align_left(left_pair, (loop_size * 2 - row_index - offset) % loop_size, loop_size)
    right_pair = align_right(
        right_pair, (loop_size * 2 - col_index - offset) % loop_size, loop_size
    )
    product_sum = jnp.zeros(
        (full_kept.shape[0], full_kept.shape[1], x_blocks.shape[2], x_blocks.shape[3]), jnp.float32
    )
    for turn_index in range(turn_count):
        if turn_index > 0:
            left_pair = from_behind((left_pair[0], left_pair[1]), "col", -1)
            right_pair = from_behind((right_pair[0], right_pair[1]), "row", -1)
        product_sum = product_sum + block_product(
            left_pair[0], left_pair[1], right_pair[0], right_pair[1], full_kept
        )
    return lax.psum_scatter(product_sum, "depth", scatter_dimension=0, tiled=True)


def solution(mesh):
    return jax.shard_map(
        per_device,
        mesh=mesh,
        in_specs=(
            P(("row", "depth"), "col", None, None),
            P(("row", "depth"), "col"),
            P(("row", "depth"), "col"),
        ),
        out_specs=P(("row", "depth"), "col", None, None),
        check_vma=False,
    )
```

profile of v0, /device:TPU:0, one launch (start us, length us, event | category | flops | bytes accessed | tf_op | source)
XLA Modules:
  0.0 470.4 jit_solution(7560682568731623647)
XLA Ops:
  7.3 16.5 %all-gather.4.cloned.1.call-done = f32[12,4,128,128]{3,2,1,0:T(8,128)} async-done(((f32[6,4,128,128]{3,2,1,0:T(8,128)}), f32[12,4,128,128]{3,2,1,0:T(8,128)}) %all-gather.4.cloned.1.call-update) | async-done | bytes 3145744 | tf_op jit(solution)/shard_map/all_gather | solution.py:52
  23.8 1.7 collective-permute-start.6
  25.5 1.5 collective-permute-start.4
  27.0 69.1 %collective-permute-done.6 = f32[12,4,128,128]{3,2,1,0:T(8,128)S(1)} collective-permute-done((f32[12,4,128,128]{3,2,1,0:T(8,128)}, f32[12,4,128,128]{3,2,1,0:T(8,128)S(1)}, u32[]{:S(2)}, u32[]{:S(2)}) %collective-permute-start.6) | collective-permute-done | bytes 3145760 | tf_op jit(solution)/shard_map/ppermute | solution.py:10
  96.1 1.7 copy-done.2
  97.8 4.8 %broadcast_select_fusion = (f32[12,4,128,128]{3,2,1,0:T(8,128)}, f32[12,4,128,128]{3,2,1,0:T(8,128)S(1)}) fusion(f32[12,4,128,128]{3,2,1,0:T(8,128)} %copy-done.2, f32[12,4,128,128]{3,2,1,0:T(8,128)} %all-gather.4.cloned.1.call-done, pred[]{:T(512)S(6)} %eq.42, f32[12,4,128,128]{3,2,1,0:T(8,128)} %collective-permute-done.4, pred[]{:T(512)S(6)} %eq.40), kind=kLoop, calls=%fused_computation.17 | loop fusion | flops 1572864 | bytes 15728642 | tf_op jit(solution)/shard_map/jit(_where)/select_n | solution.py:28
  102.6 1.7 collective-permute-start.5
  104.3 1.1 collective-permute-start.7
  105.5 1.8 all-gather
  107.3 1.9 collective-permute-start.2
  109.3 2.4 collective-permute-start
  111.7 1.8 all-gather.1
  113.7 61.4 %collective-permute-done.2 = s32[12,4]{0,1:T(4,128)S(1)} collective-permute-done((s32[12,4]{0,1:T(4,128)S(1)}, s32[12,4]{0,1:T(4,128)S(1)}, u32[]{:S(2)}, u32[]{:S(2)}) %collective-permute-start.2) | collective-permute-done | bytes 224 | tf_op jit(solution)/shard_map/ppermute | solution.py:10
  175.1 67.8 %collective-permute-start.3 = (s32[12,4]{0,1:T(4,128)S(1)}, s32[12,4]{0,1:T(4,128)S(1)}, u32[]{:S(2)}, u32[]{:S(2)}) collective-permute-start(s32[12,4]{0,1:T(4,128)S(1)} %broadcast_select_fusion.8), channel_id=1, source_target_pairs={{0,4},{2,6},{4,0},{6,2},{1,5},{3,7},{5,1},{7,3},{8,12},{10,14},{12... | collective-permute-start | bytes 584 | tf_op jit(solution)/shard_map/ppermute | solution.py:10
  243.5 1.0 collective-permute-done.3
  245.1 2.4 broadcast_select_fusion.3
  247.5 2.4 collective-permute-start.10
  249.9 4.3 broadcast_select_fusion.1
  254.1 3.9 collective-permute-start.11
  259.4 57.8 %collective-permute-done.8 = s32[12,4]{1,0:T(8,128)S(1)} collective-permute-done((s32[12,4]{1,0:T(8,128)S(1)}, s32[12,4]{1,0:T(8,128)S(1)}, u32[]{:S(2)}, u32[]{:S(2)}) %collective-permute-start.8) | collective-permute-done | bytes 224 | tf_op jit(solution)/shard_map/ppermute | solution.py:10
  317.8 5.9 %gather_fusion.1 = f32[48,4,128,128]{3,2,1,0:T(8,128)} fusion(f32[12,4,128,128]{3,2,1,0:T(8,128)S(1)} %broadcast_select_fusion.3, s32[1024]{0:T(1024)S(1)} %pad_clamp_fusion.1), kind=kCustom, calls=%fused_computation.1.clone | custom fusion | bytes 25166016 | tf_op jit(solution)/shard_map/jit(_take)/gather | solution.py:14
  323.7 12.6 %copy.41 = f32[12,4,4,128,128]{3,4,2,1,0:T(8,128)} copy(f32[12,4,4,128,128]{4,3,2,1,0:T(8,128)} %bitcast.43) | data formatting | bytes 25165824 | tf_op jit(solution)/shard_map/jit(_take)/gather | solution.py:14
  336.3 16.3 %fusion.8 = f32[12,4,4,128,128]{3,4,2,1,0:T(8,128)} fusion(f32[12,4,4,128,128]{3,4,2,1,0:T(8,128)} %copy.41, pred[12,4]{1,0:T(8,128)(4,1)S(1)} %copy.33, f32[12,4,128,128]{3,2,1,0:T(8,128)} %broadcast_select_fusion.1), kind=kOutput, calls=%fused_computation.12 | convolution fusion | flops 4834983936 | bytes 28311600 | tf_op jit(solution)/shard_map/isab,istbc->istac/dot_general | solution.py:16
  352.6 15.0 %copy.42 = f32[12,4,4,128,128]{4,2,1,3,0:T(4,128)} copy(f32[12,4,4,128,128]{3,4,2,1,0:T(8,128)} %fusion.8) | data formatting | bytes 25165824 | tf_op jit(solution)/shard_map/isab,istbc->istac/transpose | solution.py:16
  367.7 14.4 %fusion.17 = f32[12,4,128,128,1]{3,1,4,2,0:T(4,128)} fusion(f32[12,4,4,128,128]{4,2,1,3,0:T(4,128)} %copy.42, s32[12,4]{1,0:T(8,128)S(1)} %copy.38, s32[12,4,4]{2,1,0:T(4,128)S(1)} %broadcast_select_fusion.5), kind=kOutput, calls=%fused_computation.22 | convolution fusion | flops 150995712 | bytes 15729600 | tf_op jit(solution)/shard_map/istu,istac->iuac/dot_general | solution.py:20
  382.1 9.4 %gather_fusion.3 = f32[48,4,128,128]{3,2,1,0:T(8,128)} fusion(f32[12,4,128,128]{3,2,1,0:T(8,128)} %collective-permute-done.10, s32[1024]{0:T(1024)S(1)} %pad_clamp_fusion), kind=kCustom, calls=%fused_computation.3.clone | custom fusion | bytes 25166016 | tf_op jit(solution)/shard_map/jit(_take)/gather | solution.py:14
  391.5 12.6 %copy.47 = f32[12,4,4,128,128]{3,4,2,1,0:T(8,128)} copy(f32[12,4,4,128,128]{4,3,2,1,0:T(8,128)} %bitcast.42) | data formatting | bytes 25165824 | tf_op jit(solution)/shard_map/jit(_take)/gather | solution.py:14
  404.1 16.5 %fusion.11 = f32[12,4,4,128,128]{3,4,2,1,0:T(8,128)} fusion(f32[12,4,4,128,128]{3,4,2,1,0:T(8,128)} %copy.47, pred[12,4]{1,0:T(8,128)(4,1)S(1)} %copy.43, f32[12,4,128,128]{3,2,1,0:T(8,128)} %collective-permute-done.11), kind=kOutput, calls=%fused_computation.13 | convolution fusion | flops 4834983936 | bytes 28311600 | tf_op jit(solution)/shard_map/isab,istbc->istac/dot_general | solution.py:16
  420.6 15.2 %copy.48 = f32[12,4,4,128,128]{4,2,1,3,0:T(4,128)} copy(f32[12,4,4,128,128]{3,4,2,1,0:T(8,128)} %fusion.11) | data formatting | bytes 25165824 | tf_op jit(solution)/shard_map/isab,istbc->istac/transpose | solution.py:16
  435.8 13.3 %bitcast_add_fusion = f32[12,4,128,128]{3,1,2,0:T(4,128)S(1)} fusion(f32[12,4,128,128,1]{3,1,4,2,0:T(4,128)S(1)} %copy-done, f32[12,4,4,128,128]{4,2,1,3,0:T(4,128)} %copy.48, s32[12,4,4]{2,1,0:T(4,128)S(1)} %broadcast_select_fusion.4, s32[12,4]{1,0:T(8,128)S(1)} %copy.38), kind=kOutput, calls=%fused_computation.16 | convolution fusion | flops 151782144 | bytes 18875328 | tf_op jit(solution)/shard_map/istu,istac->iuac/dot_general | solution.py:20
  449.2 2.1 copy.49
  451.3 12.3 %reduce-scatter.2.cloned.1.call-done = f32[6,4,128,128]{3,2,1,0:T(8,128)} async-done(((f32[12,4,128,128]{3,2,1,0:T(8,128)}), f32[6,4,128,128]{3,2,1,0:T(8,128)}) %reduce-scatter.2.cloned.1.call-update) | async-done | bytes 1572880 | tf_op jit(solution)/shard_map/reduce_scatter | solution.py:74
  (49 shorter events, 4.3 us)
Async XLA Ops:
  6.5 17.2 %all-gather.4.cloned.1.call-start = ((), (), s32[]{:S(2)}) async-start(), calls=%async_computation.1 | async-start | bytes 4718592 | tf_op jit(solution)/shard_map/all_gather | solution.py:52
  7.3 456.3 %reduce-scatter.2.cloned.1.call-start = ((), (), s32[]{:S(2)}) async-start(), calls=%async_computation.2 | async-start | bytes 4718592 | tf_op jit(solution)/shard_map/reduce_scatter | solution.py:74
  23.8 72.4 %collective-permute-start.6 = (f32[12,4,128,128]{3,2,1,0:T(8,128)}, f32[12,4,128,128]{3,2,1,0:T(8,128)S(1)}, u32[]{:S(2)}, u32[]{:S(2)}) collective-permute-start(f32[12,4,128,128]{3,2,1,0:T(8,128)} %all-gather.4.cloned.1.call-done), channel_id=1, source_target_pairs={{0,2},{2,4},{4,6},{6,0},{1,3},{3,5},{5,7},{7,1},{8,10},{10,12},{12... | collective-permute-start | bytes 9437192 | tf_op jit(solution)/shard_map/ppermute | solution.py:10
  25.5 72.3 %collective-permute-start.4 = (f32[12,4,128,128]{3,2,1,0:T(8,128)}, f32[12,4,128,128]{3,2,1,0:T(8,128)}, u32[]{:S(2)}, u32[]{:S(2)}) collective-permute-start(f32[12,4,128,128]{3,2,1,0:T(8,128)} %all-gather.4.cloned.1.call-done), channel_id=1, source_target_pairs={{0,8},{8,16},{16,24},{24,0},{1,9},{9,17},{17,25},{25,1},{2,10},{10... | collective-permute-start | bytes 9437192 | tf_op jit(solution)/shard_map/ppermute | solution.py:10
  27.0 78.5 %copy-start.3 = (s32[6,4]{0,1:T(4,128)S(1)}, s32[6,4]{0,1:T(4,128)}, u32[]{:S(2)}) copy-start(s32[6,4]{0,1:T(4,128)} %param.8) | copy-start | bytes 292
  27.0 84.7 %copy-start.4 = (s32[6,4]{0,1:T(4,128)S(1)}, s32[6,4]{0,1:T(4,128)}, u32[]{:S(2)}) copy-start(s32[6,4]{0,1:T(4,128)} %param.9) | copy-start | bytes 292
  96.1 1.7 copy-start.2
  102.6 142.5 %copy-start.1 = (f32[12,4,128,128]{3,2,1,0:T(8,128)}, f32[12,4,128,128]{3,2,1,0:T(8,128)S(1)}, u32[]{:S(2)}) copy-start(f32[12,4,128,128]{3,2,1,0:T(8,128)S(1)} %get-tuple-element.10) | copy-start | bytes 9437188
  102.6 142.5 %collective-permute-start.5 = (f32[12,4,128,128]{3,2,1,0:T(8,128)S(1)}, f32[12,4,128,128]{3,2,1,0:T(8,128)}, u32[]{:S(2)}, u32[]{:S(2)}) collective-permute-start(f32[12,4,128,128]{3,2,1,0:T(8,128)S(1)} %get-tuple-element.10), channel_id=1, source_target_pairs={{0,16},{8,24},{16,0},{24,8},{1,17},{9,25},{17,1},{25,9},{2,18},{10... | collective-permute-start | bytes 9437192 | tf_op jit(solution)/shard_map/ppermute | solution.py:10
  104.3 145.5 %collective-permute-start.7 = (f32[12,4,128,128]{3,2,1,0:T(8,128)}, f32[12,4,128,128]{3,2,1,0:T(8,128)}, u32[]{:S(2)}, u32[]{:S(2)}) collective-permute-start(f32[12,4,128,128]{3,2,1,0:T(8,128)} %get-tuple-element.9), channel_id=1, source_target_pairs={{0,4},{2,6},{4,0},{6,2},{1,5},{3,7},{5,1},{7,3},{8,12},{10,14},{12... | collective-permute-start | bytes 9437192 | tf_op jit(solution)/shard_map/ppermute | solution.py:10
  107.3 67.8 %collective-permute-start.2 = (s32[12,4]{0,1:T(4,128)S(1)}, s32[12,4]{0,1:T(4,128)S(1)}, u32[]{:S(2)}, u32[]{:S(2)}) collective-permute-start(s32[12,4]{0,1:T(4,128)S(1)} %reshape.54), channel_id=1, source_target_pairs={{0,2},{2,4},{4,6},{6,0},{1,3},{3,5},{5,7},{7,1},{8,10},{10,12},{12... | collective-permute-start | bytes 584 | tf_op jit(solution)/shard_map/ppermute | solution.py:10
  109.3 133.6 %collective-permute-start = (s32[12,4]{1,0:T(8,128)S(1)}, s32[12,4]{1,0:T(8,128)S(1)}, u32[]{:S(2)}, u32[]{:S(2)}) collective-permute-start(s32[12,4]{1,0:T(8,128)S(1)} %copy.34), channel_id=1, source_target_pairs={{0,8},{8,16},{16,24},{24,0},{1,9},{9,17},{17,25},{25,1},{2,10},{10... | collective-permute-start | bytes 584 | tf_op jit(solution)/shard_map/ppermute | solution.py:10
  175.1 69.4 %collective-permute-start.3 = (s32[12,4]{0,1:T(4,128)S(1)}, s32[12,4]{0,1:T(4,128)S(1)}, u32[]{:S(2)}, u32[]{:S(2)}) collective-permute-start(s32[12,4]{0,1:T(4,128)S(1)} %broadcast_select_fusion.8), channel_id=1, source_target_pairs={{0,4},{2,6},{4,0},{6,2},{1,5},{3,7},{5,1},{7,3},{8,12},{10,14},{12... | collective-permute-start | bytes 584 | tf_op jit(solution)/shard_map/ppermute | solution.py:10
  243.0 15.3 %collective-permute-start.1 = (s32[12,4]{1,0:T(8,128)S(1)}, s32[12,4]{1,0:T(8,128)S(1)}, u32[]{:S(2)}, u32[]{:S(2)}) collective-permute-start(s32[12,4]{1,0:T(8,128)S(1)} %broadcast_select_fusion.6), channel_id=1, source_target_pairs={{0,16},{8,24},{16,0},{24,8},{1,17},{9,25},{17,1},{25,9},{2,18},{10... | collective-permute-start | bytes 584 | tf_op jit(solution)/shard_map/ppermute | solution.py:10
  244.5 14.5 %collective-permute-start.9 = (s32[12,4]{0,1:T(4,128)S(1)}, s32[12,4]{0,1:T(4,128)S(1)}, u32[]{:S(2)}, u32[]{:S(2)}) collective-permute-start(s32[12,4]{0,1:T(4,128)S(1)} %get-tuple-element.8), channel_id=1, source_target_pairs={{0,6},{2,0},{4,2},{6,4},{1,7},{3,1},{5,3},{7,5},{8,14},{10,8},{12,... | collective-permute-start | bytes 584 | tf_op jit(solution)/shard_map/ppermute | solution.py:10
  247.5 134.6 %collective-permute-start.10 = (f32[12,4,128,128]{3,2,1,0:T(8,128)S(1)}, f32[12,4,128,128]{3,2,1,0:T(8,128)}, u32[]{:S(2)}, u32[]{:S(2)}) collective-permute-start(f32[12,4,128,128]{3,2,1,0:T(8,128)S(1)} %broadcast_select_fusion.3), channel_id=1, source_target_pairs={{0,24},{8,0},{16,8},{24,16},{1,25},{9,1},{17,9},{25,17},{2,26},{10... | collective-permute-start | bytes 9437192 | tf_op jit(solution)/shard_map/ppermute | solution.py:10
  254.1 150.0 %collective-permute-start.11 = (f32[12,4,128,128]{3,2,1,0:T(8,128)}, f32[12,4,128,128]{3,2,1,0:T(8,128)}, u32[]{:S(2)}, u32[]{:S(2)}) collective-permute-start(f32[12,4,128,128]{3,2,1,0:T(8,128)} %broadcast_select_fusion.1), channel_id=1, source_target_pairs={{0,6},{2,0},{4,2},{6,4},{1,7},{3,1},{5,3},{7,5},{8,14},{10,8},{12,... | collective-permute-start | bytes 9437192 | tf_op jit(solution)/shard_map/ppermute | solution.py:10
  258.3 58.9 %collective-permute-start.8 = (s32[12,4]{1,0:T(8,128)S(1)}, s32[12,4]{1,0:T(8,128)S(1)}, u32[]{:S(2)}, u32[]{:S(2)}) collective-permute-start(s32[12,4]{1,0:T(8,128)S(1)} %broadcast_select_fusion.7), channel_id=1, source_target_pairs={{0,24},{8,0},{16,8},{24,16},{1,25},{9,1},{17,9},{25,17},{2,26},{10... | collective-permute-start | bytes 584 | tf_op jit(solution)/shard_map/ppermute | solution.py:10
  420.6 15.2 %copy-start = (f32[12,4,128,128,1]{3,1,4,2,0:T(4,128)S(1)}, f32[12,4,128,128,1]{3,1,4,2,0:T(4,128)}, u32[]{:S(2)}) copy-start(f32[12,4,128,128,1]{3,1,4,2,0:T(4,128)} %fusion.17) | copy-start | bytes 9437188
Sparse Core Ops, SparseCore 0:
  8.9 14.8 all-gather.3
  451.4 12.0 reduce-scatter.1
where the time goes:
time: 471 us; the launch traced here: 470 us
  waiting for transfers between devices  219 us (46%)
  starting transfers between devices  85.6 us (18%)
  local copies, waits for them, and re-layouts  76.7 us (16%)
  matrix products  60.6 us (13%)
  between operations  13.5 us (3%)
  other arithmetic  11.7 us (2%)
    ppermute x12, waiting for transfers between devices, from_behind(): return lax.ppermute(value, axis, pairs)  189 us
    ppermute x12, starting transfers between devices, from_behind(): return lax.ppermute(value, axis, pairs)  85.6 us
    gather x4, local copies, waits for them, and re-layouts, block_product(): picked = jnp.take(right_blocks, left_cols, axis=0)  40.5 us
    dot_general x2, matrix products, block_product(): jnp.einsum('isab,istbc->istac', left_blocks, picked, precision=lax.Precis...  32.8 us
    transpose x2, local copies, waits for them, and re-layouts, block_product(): jnp.einsum('isab,istbc->istac', left_blocks, picked, precision=lax.Precis...  30.2 us
    dot_general x2, matrix products, block_product(): jnp.einsum('istu,istac->iuac', matches, partial_prod, precision=lax.Preci...  27.7 us
    all_gather x1, waiting for transfers between devices, per_device(): lax.all_gather(x_blocks, 'depth', axis=0, tiled=True)  16.5 us
    reduce_scatter x1, waiting for transfers between devices, per_device(): lax.psum_scatter(product_sum, 'depth', scatter_dimension=0, tiled=True)  12.3 us
  transfers between devices with their start and end apart: 14, of which 6 were waited for; matrix products, arithmetic and copies ran while one was open for 20% of the time, Pallas kernels for 0%

commit v1 on v0

v1 whole, which is shorter than its diff:
```python
import functools

import jax
import jax.numpy as jnp
from jax import lax
from jax.experimental import pallas as pl
from jax.experimental.pallas import tpu as pltpu
from jax.sharding import PartitionSpec as P

MESH = pl.DeviceIdType.MESH


def split(value):
    high = value.astype(jnp.bfloat16)
    low = (value - high.astype(jnp.float32)).astype(jnp.bfloat16)
    return high, low


def kernel(
    sizes,
    kept_ref,
    names_ref,
    x_ref,
    out_ref,
    right,
    left,
    right_names,
    left_names,
    right_table,
    left_table,
    right_send,
    right_recv,
    core_send,
    core_recv,
    up_send,
    down_send,
    left_recv,
    rn_send,
    rn_recv,
    ln_send,
    ln_recv,
    local_sem,
):
    n_row, n_col, n_depth = sizes
    rows, slots = x_ref.shape[0], x_ref.shape[1]
    n_right = n_row * n_depth
    r, c, d = lax.axis_index("row"), lax.axis_index("col"), lax.axis_index("depth")
    me = r * n_depth + d

    def right_peer(step):
        other = lax.rem(me + step, n_right)
        return {"row": other // n_depth, "depth": lax.rem(other, n_depth)}

    barrier = pltpu.get_barrier_semaphore()
    for step in range(1, n_right):
        pl.semaphore_signal(barrier, inc=1, device_id=right_peer(step), device_id_type=MESH)
    for step in range(1, n_col):
        pl.semaphore_signal(
            barrier, inc=1, device_id={"col": lax.rem(c + step, n_col)}, device_id_type=MESH
        )
    pl.semaphore_wait(barrier, n_right + n_col - 2)

    def left_copy(source, i, sem, to):
        return pltpu.make_async_remote_copy(
            src_ref=left.at[source, i],
            dst_ref=left.at[source, i],
            send_sem=sem.at[source, i],
            recv_sem=left_recv.at[source, i],
            device_id={"col": to},
            device_id_type=MESH,
        )

    def own_left_copy(i, sem, to):
        return pltpu.make_async_remote_copy(
            src_ref=x_ref.at[i],
            dst_ref=left.at[c, i],
            send_sem=sem.at[c, i],
            recv_sem=left_recv.at[c, i],
            device_id={"col": to},
            device_id_type=MESH,
        )

    def right_copy(step):
        return pltpu.make_async_remote_copy(
            src_ref=x_ref,
            dst_ref=right_view(me),
            send_sem=right_send.at[step],
            recv_sem=right_recv.at[r],
            device_id={"row": lax.rem(r + step, n_row)},
            device_id_type=MESH,
        )

    def right_view(who):
        return right.at[pl.ds(who * rows, rows)]

    def core_copy(row, own):
        who = row * n_depth + d
        return pltpu.make_async_remote_copy(
            src_ref=x_ref if own else right_view(who),
            dst_ref=right_view(who),
            send_sem=core_send.at[row],
            recv_sem=core_recv.at[row],
            device_id={"depth": 1 - d},
            device_id_type=MESH,
        )

    def right_names_copy(step, who):
        return pltpu.make_async_remote_copy(
            src_ref=names_ref,
            dst_ref=right_names.at[who],
            send_sem=rn_send.at[step],
            recv_sem=rn_recv.at[who],
            device_id=right_peer(step),
            device_id_type=MESH,
        )

    def left_names_copy(step, who):
        return pltpu.make_async_remote_copy(
            src_ref=names_ref,
            dst_ref=left_names.at[who],
            send_sem=ln_send.at[step],
            recv_sem=ln_recv.at[who],
            device_id={"col": lax.rem(c + step, n_col)},
            device_id_type=MESH,
        )

    for i in range(rows):
        @pl.when(c < n_col - 1)
        def _():
            own_left_copy(i, up_send, c + 1).start()

        @pl.when(c > 0)
        def _():
            own_left_copy(i, down_send, c - 1).start()

    for step in range(1, n_row):
        right_copy(step).start()
    core_copy(r, True).start()
    for step in range(1, n_right):
        right_names_copy(step, me).start()
    for step in range(1, n_col):
        left_names_copy(step, c).start()
    local_right = pltpu.make_async_copy(x_ref, right_view(me), local_sem.at[0])
    local_left = pltpu.make_async_copy(x_ref, left.at[c], local_sem.at[1])
    local_rn = pltpu.make_async_copy(names_ref, right_names.at[me], local_sem.at[2])
    local_ln = pltpu.make_async_copy(names_ref, left_names.at[c], local_sem.at[3])
    for copy in (local_right, local_left, local_rn, local_ln):
        copy.start()
    right[n_right * rows] = jnp.zeros(right.shape[1:], jnp.float32)
    out_ref[...] = jnp.zeros_like(out_ref)
    for copy in (local_right, local_left, local_rn, local_ln):
        copy.wait()
    for step in range(1, n_right):
        right_names_copy(step, lax.rem(me + n_right - step, n_right)).wait_recv()
    for step in range(1, n_col):
        left_names_copy(step, lax.rem(c + n_col - step, n_col)).wait_recv()
    table_right = pltpu.make_async_copy(right_names, right_table, local_sem.at[4])
    table_left = pltpu.make_async_copy(left_names, left_table, local_sem.at[5])
    table_right.start()
    table_left.start()
    table_right.wait()
    table_left.wait()

    def compute(p, i):
        panel_rows = rows * n_depth
        for pair in range(slots // 2):
            first, second = 2 * pair, 2 * pair + 1
            whole = jnp.concatenate([left[p, i, first], left[p, i, second]], axis=1)
            l_high, l_low = split(whole)
            l_both = jnp.concatenate([l_high, l_low], axis=0)
            found = []
            for s in (first, second):
                k = left_table[p, i, s]
                upper = jnp.where(k >= rows, 1, 0)
                who, inside = p * n_depth + upper, k - upper * rows
                names = [right_table[who, inside, t] for t in range(slots)]
                base = p * panel_rows + k
                found.append((base, names))
            for half in range(slots // 2):
                cols = []
                for u in (2 * half, 2 * half + 1):
                    want = kept_ref[i, u]
                    parts = []
                    for base, names in found:
                        row, slot = n_right * rows, 0
                        for t in range(slots):
                            hit = names[t] == want
                            row = jnp.where(hit, base, row)
                            slot = jnp.where(hit, t, slot)
                        parts.append(right[row, slot])
                    cols.append(jnp.concatenate(parts, axis=0))
                r_high, r_low = split(jnp.concatenate(cols, axis=1))
                both = jnp.dot(l_both, r_high, preferred_element_type=jnp.float32)
                half_rows = whole.shape[0]
                total = both[:half_rows] + both[half_rows:]
                total += jnp.dot(l_high, r_low, preferred_element_type=jnp.float32)
                width = whole.shape[0]
                out_ref[i, 2 * half] += total[:, :width]
                out_ref[i, 2 * half + 1] += total[:, width:]

    def compute_panel(p):
        def one(i, carry):
            compute(p, i)
            return carry

        lax.fori_loop(0, rows, one, 0)

    for dist in range(1, n_col - 1):
        for i in range(rows):
            @pl.when(c - dist >= 0)
            def _():
                left_copy(c - dist, i, up_send, c).wait_recv()

                @pl.when(c < n_col - 1)
                def _():
                    left_copy(c - dist, i, up_send, c + 1).start()

            @pl.when(c + dist < n_col)
            def _():
                left_copy(c + dist, i, down_send, c).wait_recv()

                @pl.when(c > 0)
                def _():
                    left_copy(c + dist, i, down_send, c - 1).start()

    for step in range(1, n_row):
        source = lax.rem(r + n_row - step, n_row)
        pltpu.make_async_remote_copy(
            src_ref=x_ref,
            dst_ref=right_view(source * n_depth + d),
            send_sem=right_send.at[step],
            recv_sem=right_recv.at[source],
            device_id={"row": source},
            device_id_type=MESH,
        ).wait_recv()
        core_copy(source, False).start()
    for row in range(n_row):
        other = row * n_depth + 1 - d
        pltpu.make_async_remote_copy(
            src_ref=x_ref,
            dst_ref=right_view(other),
            send_sem=core_send.at[row],
            recv_sem=core_recv.at[row],
            device_id={"depth": 1 - d},
            device_id_type=MESH,
        ).wait_recv()

    compute_panel(c)
    for dist in range(1, n_col - 1):
        @pl.when(c - dist >= 0)
        def _():
            compute_panel(c - dist)

        @pl.when(c + dist < n_col)
        def _():
            compute_panel(c + dist)

    last = n_col - 1

    def finish(source, sem):
        def one(i, carry):
            left_copy(source, i, sem, c).wait_recv()
            compute(source, i)
            return carry

        lax.fori_loop(0, rows, one, 0)

    @pl.when(c == last)
    def _():
        finish(c - last, up_send)

    @pl.when(c == 0)
    def _():
        finish(c + last, down_send)

    for step in range(1, n_row):
        right_copy(step).wait_send()
    core_copy(r, True).wait_send()
    for step in range(1, n_row):
        core_copy(lax.rem(r + step, n_row), False).wait_send()
    for step in range(1, n_right):
        right_names_copy(step, me).wait_send()
    for step in range(1, n_col):
        left_names_copy(step, c).wait_send()

    def drain(i, carry):
        @pl.when(c < n_col - 1)
        def _():
            own_left_copy(i, up_send, c + 1).wait_send()
            for dist in range(1, n_col - 1):
                @pl.when(c - dist >= 0)
                def _():
                    left_copy(c - dist, i, up_send, c + 1).wait_send()

        @pl.when(c > 0)
        def _():
            own_left_copy(i, down_send, c - 1).wait_send()
            for dist in range(1, n_col - 1):
                @pl.when(c + dist < n_col)
                def _():
                    left_copy(c + dist, i, down_send, c - 1).wait_send()

        return carry

    lax.fori_loop(0, rows, drain, 0)


def per_device(sizes, x_blocks, x_cols, c_cols):
    n_row, n_col, n_depth = sizes
    rows, slots, size, _ = x_blocks.shape
    n_right = n_row * n_depth
    names = jnp.pad(x_cols, ((0, -rows % 8), (0, 128 - slots)))
    dma = pltpu.SemaphoreType.DMA
    return pl.pallas_call(
        functools.partial(kernel, sizes),
        out_shape=jax.ShapeDtypeStruct((rows, c_cols.shape[1], size, size), jnp.float32),
        in_specs=[
            pl.BlockSpec(memory_space=pltpu.SMEM),
            pl.BlockSpec(memory_space=pltpu.VMEM),
            pl.BlockSpec(memory_space=pltpu.VMEM),
        ],
        out_specs=pl.BlockSpec(memory_space=pltpu.VMEM),
        scratch_shapes=[
            pltpu.VMEM((n_right * rows + 1, slots, size, size), jnp.float32),
            pltpu.VMEM((n_col, rows, slots, size, size), jnp.float32),
            pltpu.VMEM((n_right,) + names.shape, jnp.int32),
            pltpu.VMEM((n_col,) + names.shape, jnp.int32),
            pltpu.SMEM((n_right,) + names.shape, jnp.int32),
            pltpu.SMEM((n_col,) + names.shape, jnp.int32),
            dma((n_row,)),
            dma((n_row,)),
            dma((n_row,)),
            dma((n_row,)),
            dma((n_col, rows)),
            dma((n_col, rows)),
            dma((n_col, rows)),
            dma((n_right,)),
            dma((n_right,)),
            dma((n_col,)),
            dma((n_col,)),
            dma((6,)),
        ],
        compiler_params=pltpu.CompilerParams(
            collective_id=0, has_side_effects=True, vmem_limit_bytes=56 * 1024 * 1024
        ),
    )(c_cols, names, x_blocks)


def solution(mesh):
    sizes = (mesh.shape["row"], mesh.shape["col"], mesh.shape["depth"])
    return jax.shard_map(
        functools.partial(per_device, sizes),
        mesh=mesh,
        in_specs=(
            P(("row", "depth"), "col", None, None),
            P(("row", "depth"), "col"),
            P(("row", "depth"), "col"),
        ),
        out_specs=P(("row", "depth"), "col", None, None),
        check_vma=False,
    )
```

time: 471 us -> 156 us (0.33)
  waiting for transfers between devices: 219 us -> 0 us
  Pallas kernels: 0 us -> 150 us
  starting transfers between devices: 85.6 us -> 0 us
  local copies, waits for them, and re-layouts: 76.7 us -> 5.42 us
  matrix products: 60.6 us -> 0 us
  between operations: 13.5 us -> 0.01 us
  other arithmetic: 11.7 us -> 0 us
    ppermute x12 -> x0, waiting for transfers between devices: 189 us -> none  [from_behind(): return lax.ppermute(value, axis, pairs)]
    pallas_call x0 -> x1, Pallas kernels: none -> 150 us  [per_device(): pl.pallas_call(functools.partial(kernel, sizes), out_shape=jax.ShapeDtype...]
    ppermute x12 -> x0, starting transfers between devices: 85.6 us -> none  [from_behind(): return lax.ppermute(value, axis, pairs)]
    dot_general x4 -> x0, matrix products: 60.6 us -> none  [the longest x2 32.8 us: block_product(): jnp.einsum('isab,istbc->istac', left_blocks, picked, precision=lax.Precis...]
    gather x6 -> x0, local copies, waits for them, and re-layouts: 41.7 us -> none  [the longest x4 40.5 us: block_product(): picked = jnp.take(right_blocks, left_cols, axis=0)]
    transpose x2 -> x0, local copies, waits for them, and re-layouts: 30.2 us -> none  [block_product(): jnp.einsum('isab,istbc->istac', left_blocks, picked, precision=lax.Precis...]
    all_gather x1 -> x0, waiting for transfers between devices: 16.5 us -> none  [per_device(): lax.all_gather(x_blocks, 'depth', axis=0, tiled=True)]
    reduce_scatter x1 -> x0, waiting for transfers between devices: 12.3 us -> none  [per_device(): lax.psum_scatter(product_sum, 'depth', scatter_dimension=0, tiled=True)]
  transfers between devices with their start and end apart: 14 -> 0, of which waited for: 6 -> 0; matrix products, arithmetic and copies ran while one was open for 20% -> 0% of each run, Pallas kernels for 0% -> 0%
where the time goes in v1:
time: 156 us
  Pallas kernels  150 us (96%)
  local copies, waits for them, and re-layouts  5.42 us (3%)
    pallas_call x1, Pallas kernels, per_device(): pl.pallas_call(functools.partial(kernel, sizes), out_shape=jax.ShapeDtype...  150 us
    unnamed x3, local copies, waits for them, and re-layouts  4.82 us

profile of v1, /device:TPU:0, one launch (start us, length us, event | category | flops | bytes accessed | tf_op | source)
XLA Modules:
  0.0 155.7 jit_solution(17984600922369369620)
XLA Ops:
  0.0 0.8 copy.4
  0.8 0.6 pad.4.names_ref
  1.4 1.4 copy.5.kept_ref
  2.7 150.2 %shard_map.37 = f32[6,4,128,128]{3,2,1,0:T(8,128)} custom-call(s32[6,4]{1,0:T(8,128)} %copy.5.kept_ref, s32[8,128]{1,0:T(8,128)} %pad.4.names_ref, f32[6,4,128,128]{3,2,1,0:T(8,128)} %x_ref.1), custom_call_target="tpu_custom_call" | custom-call | tf_op jit(solution)/shard_map/pallas_call | solution.py:314
  153.0 2.7 %copy.7 = f32[6,4,128,128]{3,2,1,0:T(8,128)} copy(f32[6,4,128,128]{3,2,1,0:T(8,128)} %shard_map.37) | data formatting | bytes 3145728

commit v2 on v1

v2 whole, which is shorter than its diff:
```python
import functools

import jax
import jax.numpy as jnp
from jax import lax
from jax.experimental import pallas as pl
from jax.experimental.pallas import tpu as pltpu
from jax.sharding import PartitionSpec as P

MESH = pl.DeviceIdType.MESH


def split(value):
    high = value.astype(jnp.bfloat16)
    low = (value - high.astype(jnp.float32)).astype(jnp.bfloat16)
    return high, low


def kernel(
    sizes,
    names_ref,
    x_ref,
    out_ref,
    right,
    left,
    right_names,
    left_names,
    right_table,
    left_table,
    own_send,
    pass_send,
    right_recv,
    core_send,
    core_recv,
    up_send,
    down_send,
    left_recv,
    rn_send,
    rn_recv,
    ln_send,
    ln_recv,
    local_sem,
):
    n_row, n_col, n_depth = sizes
    rows, slots = x_ref.shape[0], x_ref.shape[1]
    n_right = n_row * n_depth
    n_group = n_row // 2
    r, c, d = lax.axis_index("row"), lax.axis_index("col"), lax.axis_index("depth")
    me = r * n_depth + d
    group, parity = r // 2, lax.rem(r, 2)
    pair = group * 2 + 1 - parity

    def right_peer(step):
        other = lax.rem(me + step, n_right)
        return {"row": other // n_depth, "depth": lax.rem(other, n_depth)}

    barrier = pltpu.get_barrier_semaphore()
    for step in range(1, n_right):
        pl.semaphore_signal(barrier, inc=1, device_id=right_peer(step), device_id_type=MESH)
    for step in range(1, n_col):
        pl.semaphore_signal(
            barrier, inc=1, device_id={"col": lax.rem(c + step, n_col)}, device_id_type=MESH
        )
    pl.semaphore_wait(barrier, n_right + n_col - 2)

    def remote(src, dst, send, recv, to):
        return pltpu.make_async_remote_copy(
            src_ref=src, dst_ref=dst, send_sem=send, recv_sem=recv, device_id=to, device_id_type=MESH
        )

    def left_copy(source, i, sem, to, own=False):
        return remote(
            x_ref.at[i] if own else left.at[source, i],
            left.at[source, i],
            sem.at[source, i],
            left_recv.at[source, i],
            {"col": to},
        )

    def block_row(row, depth, i):
        return (row * n_depth + depth) * rows + i

    def right_copy(row, i, step, own):
        to = pair if step == 0 else lax.rem(group + step, n_group) * 2 + parity
        at = right.at[block_row(row, d, i)]
        sem = own_send if own else pass_send
        return remote(
            x_ref.at[i] if own else at, at, sem.at[step, i], right_recv.at[row, i], {"row": to}
        )

    def core_copy(row, depth, i, own=False):
        at = right.at[block_row(row, depth, i)]
        return remote(
            x_ref.at[i] if own else at, at, core_send.at[row, i], core_recv.at[row, i], {"depth": 1 - d}
        )

    def right_names_copy(step, who):
        return remote(names_ref, right_names.at[who], rn_send.at[step], rn_recv.at[who], right_peer(step))

    def left_names_copy(step, who):
        return remote(
            names_ref, left_names.at[who], ln_send.at[step], ln_recv.at[who], {"col": lax.rem(c + step, n_col)}
        )

    for step in range(1, n_right):
        right_names_copy(step, me).start()
    for step in range(1, n_col):
        left_names_copy(step, c).start()
    for i in range(rows):
        @pl.when(c < n_col - 1)
        def _():
            left_copy(c, i, up_send, c + 1, True).start()

        @pl.when(c > 0)
        def _():
            left_copy(c, i, down_send, c - 1, True).start()

        for step in range(n_group):
            right_copy(r, i, step, True).start()
    local_right = pltpu.make_async_copy(x_ref, right.at[pl.ds(me * rows, rows)], local_sem.at[0])
    local_left = pltpu.make_async_copy(x_ref, left.at[c], local_sem.at[1])
    local_rn = pltpu.make_async_copy(names_ref, right_names.at[me], local_sem.at[2])
    local_ln = pltpu.make_async_copy(names_ref, left_names.at[c], local_sem.at[3])
    for copy in (local_rn, local_ln, local_right, local_left):
        copy.start()
    for i in range(rows):
        core_copy(r, d, i, True).start()
    right[n_right * rows] = jnp.zeros(right.shape[1:], jnp.float32)
    out_ref[...] = jnp.zeros_like(out_ref)
    for copy in (local_right, local_left, local_rn, local_ln):
        copy.wait()

    def compute(p, i):
        panel_rows = rows * n_depth
        for pair in range(slots // 2):
            first, second = 2 * pair, 2 * pair + 1
            whole = jnp.concatenate([left[p, i, first], left[p, i, second]], axis=1)
            l_high, l_low = split(whole)
            l_both = jnp.concatenate([l_high, l_low], axis=0)
            found = []
            for s in (first, second):
                k = left_table[p, i, s]
                upper = jnp.where(k >= rows, 1, 0)
                who, inside = p * n_depth + upper, k - upper * rows
                names = [right_table[who, inside, t] for t in range(slots)]
                base = p * panel_rows + k
                found.append((base, names))
            for half in range(slots // 2):
                cols = []
                for u in (2 * half, 2 * half + 1):
                    want = right_table[me, i, slots + u]
                    parts = []
                    for base, names in found:
                        row, slot = n_right * rows, 0
                        for t in range(slots):
                            hit = names[t] == want
                            row = jnp.where(hit, base, row)
                            slot = jnp.where(hit, t, slot)
                        parts.append(right[row, slot])
                    cols.append(jnp.concatenate(parts, axis=0))
                r_high, r_low = split(jnp.concatenate(cols, axis=1))
                both = jnp.dot(l_both, r_high, preferred_element_type=jnp.float32)
                half_rows = whole.shape[0]
                total = both[:half_rows] + both[half_rows:]
                total += jnp.dot(l_high, r_low, preferred_element_type=jnp.float32)
                width = whole.shape[0]
                out_ref[i, 2 * half] += total[:, :width]
                out_ref[i, 2 * half + 1] += total[:, width:]

    def compute_panel(p):
        def one(i, carry):
            compute(p, i)
            return carry

        lax.fori_loop(0, rows, one, 0)

    def pass_left(dist, i):
        @pl.when(c - dist >= 0)
        def _():
            left_copy(c - dist, i, up_send, c).wait_recv()

            @pl.when(c < n_col - 1)
            def _():
                left_copy(c - dist, i, up_send, c + 1).start()

        @pl.when(c + dist < n_col)
        def _():
            left_copy(c + dist, i, down_send, c).wait_recv()

            @pl.when(c > 0)
            def _():
                left_copy(c + dist, i, down_send, c - 1).start()

    for i in range(rows):
        pass_left(1, i)
        right_copy(pair, i, 0, True).wait_recv()
        for step in range(1, n_group):
            right_copy(pair, i, step, False).start()
        core_copy(pair, d, i).start()
    for step in range(1, n_group):
        there = lax.rem(group + n_group - step, n_group) * 2
        for i in range(rows):
            right_copy(there + parity, i, step, True).wait_recv()
            core_copy(there + parity, d, i).start()
        for i in range(rows):
            if step == 1:
                pass_left(2, i)
            right_copy(there + 1 - parity, i, step, False).wait_recv()
            core_copy(there + 1 - parity, d, i).start()
    for dist in range(3, n_col - 1):
        for i in range(rows):
            pass_left(dist, i)

    for step in range(1, n_right):
        right_names_copy(step, lax.rem(me + n_right - step, n_right)).wait_recv()
    for step in range(1, n_col):
        left_names_copy(step, lax.rem(c + n_col - step, n_col)).wait_recv()
    table_right = pltpu.make_async_copy(right_names, right_table, local_sem.at[4])
    table_left = pltpu.make_async_copy(left_names, left_table, local_sem.at[5])
    table_right.start()
    table_left.start()
    table_right.wait()
    table_left.wait()
    for row in range(n_row):
        for i in range(rows):
            core_copy(row, 1 - d, i).wait_recv()

    compute_panel(c)
    for dist in range(1, n_col - 1):
        @pl.when(c - dist >= 0)
        def _():
            compute_panel(c - dist)

        @pl.when(c + dist < n_col)
        def _():
            compute_panel(c + dist)

    last = n_col - 1

    def finish(source, sem):
        def one(i, carry):
            left_copy(source, i, sem, c).wait_recv()
            compute(source, i)
            return carry

        lax.fori_loop(0, rows, one, 0)

    @pl.when(c == last)
    def _():
        finish(c - last, up_send)

    @pl.when(c == 0)
    def _():
        finish(c + last, down_send)

    for step in range(1, n_right):
        right_names_copy(step, me).wait_send()
    for step in range(1, n_col):
        left_names_copy(step, c).wait_send()

    def drain(i, carry):
        for step in range(n_group):
            right_copy(r, i, step, True).wait_send()
        for step in range(1, n_group):
            right_copy(pair, i, step, False).wait_send()
        for row in range(n_row):
            core_copy(row, d, i).wait_send()

        @pl.when(c < n_col - 1)
        def _():
            left_copy(c, i, up_send, c + 1).wait_send()
            for dist in range(1, n_col - 1):
                @pl.when(c - dist >= 0)
                def _():
                    left_copy(c - dist, i, up_send, c + 1).wait_send()

        @pl.when(c > 0)
        def _():
            left_copy(c, i, down_send, c - 1).wait_send()
            for dist in range(1, n_col - 1):
                @pl.when(c + dist < n_col)
                def _():
                    left_copy(c + dist, i, down_send, c - 1).wait_send()

        return carry

    lax.fori_loop(0, rows, drain, 0)


def per_device(sizes, x_blocks, x_cols, c_cols):
    n_row, n_col, n_depth = sizes
    rows, slots, size, _ = x_blocks.shape
    n_right = n_row * n_depth
    kept = c_cols.shape[1]
    names = jnp.concatenate([x_cols, c_cols], axis=1)
    names = jnp.pad(names, ((0, -rows % 8), (0, 128 - slots - kept)))
    dma = pltpu.SemaphoreType.DMA
    return pl.pallas_call(
        functools.partial(kernel, sizes),
        out_shape=jax.ShapeDtypeStruct((rows, kept, size, size), jnp.float32),
        in_specs=[
            pl.BlockSpec(memory_space=pltpu.VMEM),
            pl.BlockSpec(memory_space=pl.ANY),
        ],
        out_specs=pl.BlockSpec(memory_space=pltpu.VMEM),
        scratch_shapes=[
            pltpu.VMEM((n_right * rows + 1, slots, size, size), jnp.float32),
            pltpu.VMEM((n_col, rows, slots, size, size), jnp.float32),
            pltpu.VMEM((n_right,) + names.shape, jnp.int32),
            pltpu.VMEM((n_col,) + names.shape, jnp.int32),
            pltpu.SMEM((n_right,) + names.shape, jnp.int32),
            pltpu.SMEM((n_col,) + names.shape, jnp.int32),
            dma((n_row // 2, rows)),
            dma((n_row // 2, rows)),
            dma((n_row, rows)),
            dma((n_row, rows)),
            dma((n_row, rows)),
            dma((n_col, rows)),
            dma((n_col, rows)),
            dma((n_col, rows)),
            dma((n_right,)),
            dma((n_right,)),
            dma((n_col,)),
            dma((n_col,)),
            dma((6,)),
        ],
        compiler_params=pltpu.CompilerParams(
            collective_id=0, has_side_effects=True, vmem_limit_bytes=56 * 1024 * 1024
        ),
    )(names, x_blocks)


def solution(mesh):
    sizes = (mesh.shape["row"], mesh.shape["col"], mesh.shape["depth"])
    return jax.shard_map(
        functools.partial(per_device, sizes),
        mesh=mesh,
        in_specs=(
            P(("row", "depth"), "col", None, None),
            P(("row", "depth"), "col"),
            P(("row", "depth"), "col"),
        ),
        out_specs=P(("row", "depth"), "col", None, None),
        check_vma=False,
    )
```

time: 156 us -> 117 us (0.75)
  Pallas kernels: 150 us -> 112 us
    pallas_call x1, Pallas kernels: 150 us -> 112 us  [per_device(): pl.pallas_call(functools.partial(kernel, sizes), out_shape=jax.ShapeDtype...]
where the time goes in v2:
time: 117 us
  Pallas kernels  112 us (96%)
  local copies, waits for them, and re-layouts  4.84 us (4%)
    pallas_call x1, Pallas kernels, per_device(): pl.pallas_call(functools.partial(kernel, sizes), out_shape=jax.ShapeDtype...  112 us
    unnamed x3, local copies, waits for them, and re-layouts  4.24 us

profile of v2, /device:TPU:0, one launch (start us, length us, event | category | flops | bytes accessed | tf_op | source)
XLA Modules:
  0.0 117.2 jit_solution(9572772669226768485)
XLA Ops:
  0.0 0.8 copy.4
  0.8 0.8 copy.5
  1.5 0.1 pad_add_fusion
  1.6 0.6 pad.4.names_ref
  2.2 112.3 %shard_map.37 = f32[6,4,128,128]{3,2,1,0:T(8,128)} custom-call(s32[8,128]{1,0:T(8,128)} %pad.4.names_ref, f32[6,4,128,128]{3,2,1,0:T(8,128)} %x_ref.1), custom_call_target="tpu_custom_call" | custom-call | tf_op jit(solution)/shard_map/pallas_call | solution.py:298
  114.5 2.7 %copy.7 = f32[6,4,128,128]{3,2,1,0:T(8,128)} copy(f32[6,4,128,128]{3,2,1,0:T(8,128)} %shard_map.37) | data formatting | bytes 3145728
